TPU v7x, 256 devices: a whole 4x4x8 slice. The times are simulated.
256 devices in a mesh: seq: 64 (over x, z, core), head: 4 (over y).
Axes of the slice: x: 4, y: 4, z: 8, core: 2. Of those that a mesh axis runs over, the one named last changes fastest.
Arguments:
- queries: bfloat16 [65536, 2048], P('seq', 'head'), may hold values from -1.796875 to 1.796875
- keys: bfloat16 [65536, 2048], P('seq', 'head'), may hold values from -1.796875 to 1.796875
- values: bfloat16 [65536, 2048], P('seq', 'head'), may hold values from -16 to 16
- grad_out: bfloat16 [65536, 2048], P('seq', 'head'), may hold values from -1.1953125 to 1.1953125
Outputs:
- output: bfloat16 [65536, 2048], P('seq', 'head')
- grad_query: bfloat16 [65536, 2048], P('seq', 'head')
- grad_key: bfloat16 [65536, 2048], P('seq', 'head')
- grad_value: bfloat16 [65536, 2048], P('seq', 'head')
All inputs are finite; a program needn't handle non-finite values.
Results may differ from a plain program's by a relative error of at most 0.0065.
Values sent between devices are 32-bit elements; how exact they have to be, the bound alone decides.
A program may use at most 128 MiB of HBM per device.

v0:
```python
import jax
import jax.numpy as jnp
from jax import lax
from jax.sharding import PartitionSpec as P

HEADS = 16
HEAD_DIM = 128


EPSILON = 1e-06


def entering(shard, axis, combine, identity, reverse):
    size, here = (lax.axis_size(axis), lax.axis_index(axis))
    everything = lax.all_gather(shard, axis)
    start = jnp.broadcast_to(jnp.asarray(identity, shard.dtype), shard.shape)

    def step(k, before):
        at = size - 1 - k if reverse else k
        reached = at > here if reverse else at < here
        new = combine(before, everything[at])
        return jnp.where(reached, new, before)

    return lax.fori_loop(0, size, step, start)


def add_states(earlier, later):
    return earlier + later


def masked_scores(query_side, key_side):
    raw_scores = jnp.einsum(
        "thd,shd->hts", query_side, key_side, preferred_element_type=jnp.float32
    )
    count = query_side.shape[0]
    row_index = lax.broadcasted_iota(jnp.int32, (count, count), 0)
    col_index = lax.broadcasted_iota(jnp.int32, (count, count), 1)
    keep = (row_index >= col_index)[None]
    return jnp.where(keep, raw_scores, jnp.zeros_like(raw_scores)).astype(jnp.bfloat16)


def shards(queries, keys, values, grad_out):
    tok_rows = queries.shape[0]
    local_heads = queries.shape[1] // HEAD_DIM
    shaped = (tok_rows, local_heads, HEAD_DIM)
    full_width = HEADS * HEAD_DIM
    query_rows = queries.reshape(shaped)
    key_rows = keys.reshape(shaped)
    value_rows = values.reshape(shaped)
    local_state = jnp.einsum(
        "thd,the->hde", key_rows, value_rows, preferred_element_type=jnp.float32
    )
    zero_state = jnp.zeros_like(local_state)
    prefix = entering(local_state, "seq", add_states, zero_state, False)
    scores = masked_scores(query_rows, key_rows)
    prefix_round = prefix.astype(jnp.bfloat16)
    mixed = jnp.einsum("hts,she->the", scores, value_rows, preferred_element_type=jnp.float32)
    mixed = mixed + jnp.einsum(
        "thd,hde->the", query_rows, prefix_round, preferred_element_type=jnp.float32
    )
    mixed_rows = mixed.reshape(tok_rows, -1)
    grad_float = grad_out.astype(jnp.float32)
    squares = lax.psum(jnp.sum(mixed_rows * mixed_rows, axis=1), "head")
    inverse_rms = lax.rsqrt(squares / full_width + EPSILON)
    normed = mixed_rows * inverse_rms[:, None]
    crossed = lax.psum(jnp.sum(grad_float * normed, axis=1), "head")
    cross_mean = (crossed / full_width)[:, None]
    output = normed.astype(jnp.bfloat16)
    grad_mixed = (
        (inverse_rms[:, None] * (grad_float - normed * cross_mean))
        .astype(jnp.bfloat16)
        .reshape(shaped)
    )
    grad_state = jnp.einsum(
        "thd,the->hde", query_rows, grad_mixed, preferred_element_type=jnp.float32
    )
    suffix = entering(grad_state, "seq", add_states, zero_state, True)
    suffix_round = suffix.astype(jnp.bfloat16)
    grad_scores = masked_scores(grad_mixed, value_rows)
    grad_q = jnp.einsum("hts,shd->thd", grad_scores, key_rows, preferred_element_type=jnp.float32)
    grad_q = grad_q + jnp.einsum(
        "the,hde->thd", grad_mixed, prefix_round, preferred_element_type=jnp.float32
    )
    grad_k = jnp.einsum("hts,thd->shd", grad_scores, query_rows, preferred_element_type=jnp.float32)
    grad_k = grad_k + jnp.einsum(
        "she,hde->shd", value_rows, suffix_round, preferred_element_type=jnp.float32
    )
    grad_v = jnp.einsum("hts,the->she", scores, grad_mixed, preferred_element_type=jnp.float32)
    grad_v = grad_v + jnp.einsum(
        "shd,hde->she", key_rows, suffix_round, preferred_element_type=jnp.float32
    )
    flat_shape = (tok_rows, local_heads * HEAD_DIM)
    return (
        output,
        grad_q.astype(jnp.bfloat16).reshape(flat_shape),
        grad_k.astype(jnp.bfloat16).reshape(flat_shape),
        grad_v.astype(jnp.bfloat16).reshape(flat_shape),
    )


def solution(mesh):
    return jax.shard_map(
        shards,
        mesh=mesh,
        in_specs=(P("seq", "head"), P("seq", "head"), P("seq", "head"), P("seq", "head")),
        out_specs=(P("seq", "head"), P("seq", "head"), P("seq", "head"), P("seq", "head")),
        check_vma=False,
    )
```

profile of v0, /device:TPU:1, one launch (start us, length us, event | category | flops | bytes accessed | tf_op | source)
XLA Modules:
  0.0 399.9 jit_solution(9009849528236782950)
XLA Ops:
  7.2 2.4 copy.100
  9.6 2.4 fusion.10
  13.5 2.5 select_convert_fusion.1
  16.0 3.2 copy-done.1
  19.3 2.9 fusion.5
  22.2 94.0 %all-gather.5.cloned.1.call-done = f32[256,128,128]{2,1,0:T(8,128)} async-done(((f32[4,128,128]{2,1,0:T(8,128)}), f32[256,128,128]{2,1,0:T(8,128)}) %all-gather.5.cloned.1.call-update) | async-done | bytes 16777232 | tf_op jit(solution)/shard_map/all_gather | solution.py:15
  116.2 68.1 %while.30 = (s32[]{:T(128)}, f32[4,128,128]{2,1,0:T(8,128)S(1)}, s32[]{:T(128)}, f32[64,4,128,128]{3,2,1,0:T(8,128)}, s32[]{:T(128)}, /*index=5*/s32[]{:T(128)}) while((s32[]{:T(128)}, f32[4,128,128]{2,1,0:T(8,128)S(1)}, s32[]{:T(128)}, f32[64,4,128,128]{3,2,1,0:T(8,128)}, s32[]{:T(128)}, /*index=5*/s32[]{:T(128)}) %tuple.87), condition=%wide.region_1.2_spmd.clone, body=%wide.region_0.1_spmd.clone.sunk | while | flops 196612 | bytes 786533 | solution.py:24
  117.2 1.0 add_select_fusion.4
  119.3 1.0 add_select_fusion.4
  121.5 1.0 add_select_fusion.4
  123.6 1.0 add_select_fusion.4
  125.7 1.0 add_select_fusion.4
  127.9 1.0 add_select_fusion.4
  137.4 1.0 add_select_fusion.4
  139.6 1.0 add_select_fusion.4
  141.7 1.0 add_select_fusion.4
  143.8 1.0 add_select_fusion.4
  146.0 1.0 add_select_fusion.4
  148.1 1.0 add_select_fusion.4
  157.7 1.0 add_select_fusion.4
  159.8 1.0 add_select_fusion.4
  161.9 1.0 add_select_fusion.4
  164.0 1.0 add_select_fusion.4
  166.2 1.0 add_select_fusion.4
  168.3 1.0 add_select_fusion.4
  177.9 1.0 add_select_fusion.4
  180.0 1.0 add_select_fusion.4
  182.1 1.0 add_select_fusion.4
  184.3 1.8 multiply_reduce_fusion
  186.1 8.4 %psum.14 = f32[1024]{0:T(1024)S(1)} all-reduce(f32[1024]{0:T(1024)S(1)} %get-tuple-element.255), channel_id=1, replica_groups=mesh['seq'=64,'head'=4] {'head'}, use_global_device_ids=true, to_apply=%region_3.4 | all-reduce | flops 1024 | bytes 8192 | tf_op jit(solution)/shard_map/psum | solution.py:63
  194.5 1.9 copy.38
  196.5 1.7 fusion
  198.2 6.0 %psum.15 = f32[1024]{0:T(1024)S(1)} all-reduce(f32[1024]{0:T(1024)S(1)} %fusion), channel_id=1, replica_groups=mesh['seq'=64,'head'=4] {'head'}, use_global_device_ids=true, to_apply=%region_5.6 | all-reduce | flops 1024 | bytes 8192 | tf_op jit(solution)/shard_map/psum | solution.py:66
  204.2 3.0 fusion.2
  207.2 1.5 copy.56
  210.0 4.3 %select_convert_fusion = bf16[4,1024,1024]{2,1,0:T(8,128)(2,1)S(1)} fusion(bf16[1024,4,128]{0,2,1:T(8,128)(2,1)S(1)} %bitcast.105, pred[1024,1024]{1,0:T(8,128)(4,1)} %copy-done.10, bf16[1024,512]{1,0:T(8,128)(2,1)} %param.10), kind=kOutput, calls=%fused_computation.2 | convolution fusion | flops 1082130432 | bytes 11534336 | tf_op jit(solution)/shard_map/thd,shd->hts/dot_general | solution.py:32
  214.4 2.9 fusion.32
  217.6 1.4 fusion.4
  219.0 2.3 copy.51
  221.3 6.2 %fusion.33 = f32[4,128,1024]{2,1,0:T(8,128)} fusion(bf16[1024,4,128]{0,2,1:T(8,128)(2,1)S(1)} %bitcast.107, bf16[4,1024,1024]{2,1,0:T(8,128)(2,1)} %copy-done.1), kind=kOutput, calls=%fused_computation.49 | convolution fusion | flops 1073741824 | bytes 11534336 | tf_op jit(solution)/shard_map/hts,the->she/dot_general | solution.py:88
  227.5 82.1 %all-gather.7.cloned.1.call-done = f32[256,128,128]{2,1,0:T(8,128)} async-done(((f32[4,128,128]{2,1,0:T(8,128)}), f32[256,128,128]{2,1,0:T(8,128)}) %all-gather.7.cloned.1.call-update) | async-done | bytes 16777232 | tf_op jit(solution)/shard_map/all_gather | solution.py:15
  309.6 68.4 %while.31 = (s32[]{:T(128)}, f32[4,128,128]{2,1,0:T(8,128)S(1)}, s32[]{:T(128)}, f32[64,4,128,128]{3,2,1,0:T(8,128)}, s32[]{:T(128)}, /*index=5*/s32[]{:T(128)}, s32[]{:T(128)}, s32[]{:T(128)}) while((s32[]{:T(128)}, f32[4,128,128]{2,1,0:T(8,128)S(1)}, s32[]{:T(128)}, f32[64,4,128,128]{3,2,1,0:T(8,128)}, s32[]{:T(128)}, ...), condition=%wide.region_7.8_spmd.clone, body=%wide.region_6.7_spmd.clone.sunk | while | flops 196616 | bytes 786595 | solution.py:24
  310.7 1.0 add_select_fusion.5
  378.0 3.2 fusion.7
  381.2 1.5 add_convert_fusion
  382.7 2.4 copy.53
  385.1 5.7 %fusion.3 = bf16[1024,4,128]{0,2,1:T(8,128)(2,1)} fusion(f32[4,128,1024]{2,1,0:T(8,128)S(1)} %copy-done.4, bf16[4,1024,1024]{2,1,0:T(8,128)(2,1)} %copy-done.2, bf16[1024,512]{1,0:T(8,128)(2,1)S(1)} %copy-done), kind=kOutput, calls=%fused_computation.11 | convolution fusion | flops 1074790400 | bytes 12582912 | tf_op jit(solution)/shard_map/hts,thd->shd/dot_general | solution.py:84
  390.8 2.3 copy.52
  (138 shorter events, 113.3 us)
Async XLA Ops:
  7.2 6.3 %copy-start = (bf16[1024,512]{1,0:T(8,128)(2,1)S(1)}, bf16[1024,512]{1,0:T(8,128)(2,1)}, u32[]{:S(2)}) copy-start(bf16[1024,512]{1,0:T(8,128)(2,1)} %param.8) | copy-start | bytes 3145732
  7.2 2.5 copy-start.7
  7.2 109.0 %all-gather.5.cloned.1.call-start = ((), (), s32[]{:S(2)}) async-start(), calls=%async_computation | async-start | bytes 17039360 | tf_op jit(solution)/shard_map/all_gather | solution.py:15
  9.6 3.8 copy-start.5
  12.1 297.5 %all-gather.7.cloned.1.call-start = ((), (), s32[]{:S(2)}) async-start(), calls=%async_computation.1 | async-start | bytes 17039360 | tf_op jit(solution)/shard_map/all_gather | solution.py:15
  12.5 1.0 copy-start.10
  13.5 5.8 %copy-start.8 = (bf16[1024,512]{1,0:T(8,128)(2,1)S(1)}, bf16[1024,512]{1,0:T(8,128)(2,1)}, u32[]{:S(2)}) copy-start(bf16[1024,512]{1,0:T(8,128)(2,1)} %param.10) | copy-start | bytes 3145732
  16.0 3.2 copy-start.1
  210.0 4.4 %copy-start.9 = (bf16[1024,512]{0,1:T(8,128)(2,1)S(1)}, bf16[1024,512]{0,1:T(8,128)(2,1)}, u32[]{:S(2)}) copy-start(bf16[1024,512]{0,1:T(8,128)(2,1)} %copy.100) | copy-start | bytes 3145732
  214.4 3.2 copy-start.2
  378.0 3.2 copy-start.3
  378.0 3.2 copy-start.6
  382.7 2.4 copy-start.4
Sparse Core Ops, SparseCore 0:
  12.2 103.8 all-gather.4
  210.1 99.4 all-gather.6
where the time goes:
time: 404 us; the launch traced here: 400 us
  waiting for transfers between devices  176 us (44%)
  other arithmetic  138 us (34%)
  matrix products  35.3 us (9%)
  local copies, waits for them, and re-layouts  18.2 us (5%)
  blocking collectives  14.4 us (4%)
  between operations  14.2 us (4%)
    all_gather x2, waiting for transfers between devices, entering(): everything = lax.all_gather(shard, axis)  176 us
    select_n x128, other arithmetic, step(): return jnp.where(reached, new, before)  133 us
    unnamed x25, local copies, waits for them, and re-layouts  11.5 us
    psum x1, blocking collectives, shards(): squares = lax.psum(jnp.sum(mixed_rows * mixed_rows, axis=1), 'head')  8.42 us
  transfers between devices with their start and end apart: 2, of which 2 were waited for; matrix products, arithmetic and copies ran while one was open for 6% of the time, Pallas kernels for 0%

commit v1 on v0

v1 whole, which is shorter than its diff:
```python
import functools

import jax
import jax.numpy as jnp
from jax import lax
from jax.experimental import pallas as pl
from jax.experimental.pallas import tpu as pltpu
from jax.sharding import PartitionSpec as P

HEADS = 16
HEAD_DIM = 128
EPSILON = 1e-06
CHIPS_X = 4
CHUNK = 256
MESH = pl.DeviceIdType.MESH
F32 = jnp.float32
BF16 = jnp.bfloat16


def nn(a, b):
    return lax.dot_general(a, b, (((1,), (0,)), ((), ())), preferred_element_type=F32)


def nt(a, b):
    return lax.dot_general(a, b, (((1,), (1,)), ((), ())), preferred_element_type=F32)


def tn(a, b):
    return lax.dot_general(a, b, (((0,), (0,)), ((), ())), preferred_element_type=F32)


def split2(v):
    hi = v.astype(BF16)
    return hi, (v - hi.astype(F32)).astype(BF16)


def kernel(
    chips_z, n_head,
    q_hbm, k_hbm, v_hbm, g_hbm,
    o_hbm, gq_hbm, gk_hbm, gv_hbm,
    q, k, v, g, qt, mixed, gm, score_t, gk_part, gv_part, o_v, gq_v, gk_v, gv_v,
    cum, gs_part, st, cx, ps, rb, ds, rd, cs, full, diag, ysend, yrecv,
    load_sem, out_sem, core_send, core_recv, b_send, b_recv, d_send, d_recv, y_send_sem, y_recv_sem,
):
    tokens, width = q.shape
    n_local = width // HEAD_DIM
    n_pair = n_local // 2
    half_rows = n_pair * HEAD_DIM
    n_chunk = tokens // CHUNK
    n_chip = CHIPS_X * chips_z
    full_width = n_local * n_head * HEAD_DIM

    seq = lax.axis_index("seq")
    row = lax.axis_index("head")
    core = lax.rem(seq, 2)
    other = 1 - core
    chip = seq // 2
    x = chip // chips_z
    z = lax.rem(chip, chips_z)

    def far(n, d):
        return min(d, n - d)

    offsets = [(dx, dz) for dx in range(CHIPS_X) for dz in range(chips_z) if dx or dz]
    offsets.sort(key=lambda o: (-far(chips_z, o[1]), -far(CHIPS_X, o[0])))
    peers = [lax.rem(x + dx, CHIPS_X) * chips_z + lax.rem(z + dz, chips_z) for dx, dz in offsets]
    rows_of = [lax.rem(row + d, n_head) for d in range(1, n_head)]

    barrier = pltpu.get_barrier_semaphore()
    for p in peers:
        pl.semaphore_signal(barrier, inc=1, device_id=(p * 2 + core, row), device_id_type=MESH)
    for r in rows_of:
        pl.semaphore_signal(barrier, inc=1, device_id=(seq, r), device_id_type=MESH)
    pl.semaphore_signal(barrier, inc=1, device_id=(chip * 2 + other, row), device_id_type=MESH)

    loads = [
        pltpu.make_async_copy(src, dst, load_sem.at[i])
        for i, (src, dst) in enumerate(((k_hbm, k), (v_hbm, v), (q_hbm, q), (g_hbm, g)))
    ]
    for copy in loads:
        copy.start()

    def rows(j):
        return pl.ds(j * CHUNK, CHUNK) if isinstance(j, int) else pl.ds(pl.multiple_of(j * CHUNK, CHUNK), CHUNK)

    def cols(h):
        return pl.ds(h * HEAD_DIM, HEAD_DIM)

    def pair_cols(p):
        return pl.ds(p * 2 * HEAD_DIM, 2 * HEAD_DIM)

    own_rows = pl.ds(pl.multiple_of(core * half_rows, half_rows), half_rows)
    other_rows = pl.ds(pl.multiple_of(other * half_rows, half_rows), half_rows)

    row_id = lax.broadcasted_iota(jnp.int32, (CHUNK, CHUNK), 0)
    col_id = lax.broadcasted_iota(jnp.int32, (CHUNK, CHUNK), 1)

    def lower(s):
        return jnp.where(row_id >= col_id, s, 0.0).astype(BF16)

    def upper(s):
        return jnp.where(row_id <= col_id, s, 0.0).astype(BF16)

    def core_copy(s, stage):
        if stage == 0:
            src, dst = st.at[s, other_rows], cx.at[s]
        else:
            src, dst = cs.at[s], full.at[s, own_rows]
        return pltpu.make_async_remote_copy(
            src_ref=src, dst_ref=dst, send_sem=core_send.at[s, stage], recv_sem=core_recv.at[s, stage],
            device_id=(chip * 2 + other, row), device_id_type=MESH,
        )

    def to_owners(s):
        core_copy(s, 0).wait_recv()
        ps[s] = (st[s, own_rows, :] + cx[s]).reshape(ps.shape[1:])
        for p in peers:
            pltpu.make_async_remote_copy(
                src_ref=ps.at[s, p], dst_ref=rb.at[s, chip], send_sem=b_send.at[s], recv_sem=b_recv.at[s],
                device_id=(p * 2 + core, row), device_id_type=MESH,
            ).start()
        rb[s, chip] = ps[s, chip]

    def wait_all(ref, s, sem):
        part = ref.at[s, pl.ds(0, n_chip - 1)]
        pltpu.make_async_copy(part, part, sem.at[s]).wait()

    def from_owners(s):
        wait_all(rb, s, b_recv)
        total = jnp.zeros(rb.shape[2:], F32)
        for i in range(n_chip) if s == 0 else range(n_chip - 1, -1, -1):
            ds[s, i] = total
            total = total + rb[s, i]
        for p in peers:
            pltpu.make_async_remote_copy(
                src_ref=ds.at[s, p], dst_ref=rd.at[s, chip], send_sem=d_send.at[s], recv_sem=d_recv.at[s],
                device_id=(p * 2 + core, row), device_id_type=MESH,
            ).start()
        rd[s, chip] = ds[s, chip]

    def between_cores(s):
        wait_all(rd, s, d_recv)
        half = rd[s].reshape(half_rows, HEAD_DIM)
        first = core == s
        cs[s] = jnp.where(first, half + st[s, own_rows, :], half)
        full[s, own_rows, :] = jnp.where(first, half, half + cx[s])
        core_copy(s, 1).start()

    def fill_diag(s):
        for p in range(n_pair):
            for i in range(2):
                block = full[s, pl.ds((2 * p + i) * HEAD_DIM, HEAD_DIM), :].astype(BF16)
                diag[s, p, pl.ds(i * HEAD_DIM, HEAD_DIM), pl.ds(i * HEAD_DIM, HEAD_DIM)] = block

    diag[...] = jnp.zeros_like(diag)

    loads[0].wait()
    loads[1].wait()
    for h in range(n_local):
        total = None
        for j in range(n_chunk):
            if j:
                cum[j, pl.ds(h * HEAD_DIM, HEAD_DIM), :] = total
            new = tn(k[rows(j), cols(h)], v[rows(j), cols(h)])
            total = new if total is None else total + new
        cum[0, pl.ds(h * HEAD_DIM, HEAD_DIM), :] = jnp.zeros_like(total)
        st[0, pl.ds(h * HEAD_DIM, HEAD_DIM), :] = total

    pl.semaphore_wait(barrier, len(peers) + len(rows_of) + 1)
    core_copy(0, 0).start()
    loads[2].wait()
    for h in range(n_local):
        for j in range(n_chunk):
            qt[pl.ds(h * HEAD_DIM, HEAD_DIM), rows(j)] = q[rows(j), cols(h)].T
    to_owners(0)

    @pl.loop(0, n_chunk)
    def _(j):
        for h in range(n_local):
            q_c, k_c, v_c = q[rows(j), cols(h)], k[rows(j), cols(h)], v[rows(j), cols(h)]
            before = cum[j, pl.ds(h * HEAD_DIM, HEAD_DIM), :].astype(BF16)
            mixed[rows(j), cols(h)] = nn(lower(nt(q_c, k_c)), v_c) + nn(q_c, before)

    from_owners(0)

    @pl.loop(0, n_chunk)
    def _(j):
        for h in range(n_local):
            score_t[j, h] = upper(nt(k[rows(j), cols(h)], q[rows(j), cols(h)]))

    loads[3].wait()
    between_cores(0)
    core_copy(0, 1).wait_recv()
    fill_diag(0)

    sums = jnp.zeros((2 * n_chunk, CHUNK), F32)
    pick = lax.broadcasted_iota(jnp.int32, (2 * n_chunk, HEAD_DIM), 0)
    for j in range(n_chunk):
        squares = jnp.zeros((CHUNK, HEAD_DIM), F32)
        cross = jnp.zeros((CHUNK, HEAD_DIM), F32)
        for p in range(n_pair):
            m = mixed[rows(j), pair_cols(p)] + nn(q[rows(j), pair_cols(p)], diag[0, p])
            mixed[rows(j), pair_cols(p)] = m
            s2 = m * m
            sg = m * g[rows(j), pair_cols(p)].astype(F32)
            squares += s2[:, :HEAD_DIM] + s2[:, HEAD_DIM:]
            cross += sg[:, :HEAD_DIM] + sg[:, HEAD_DIM:]
        for value, at in ((squares, j), (cross, n_chunk + j)):
            one = jnp.where(pick == at, 1.0, 0.0).astype(BF16)
            for piece in split2(value):
                sums += nt(one, piece)
    ysend[...] = sums
    ycopies = [
        pltpu.make_async_remote_copy(
            src_ref=ysend, dst_ref=yrecv.at[row], send_sem=y_send_sem.at[i], recv_sem=y_recv_sem,
            device_id=(seq, r), device_id_type=MESH,
        )
        for i, r in enumerate(rows_of)
    ]
    for copy in ycopies:
        copy.start()
    yrecv[row] = sums
    part = yrecv.at[pl.ds(0, n_head - 1)]
    pltpu.make_async_copy(part, part, y_recv_sem).wait()
    sums = yrecv[0]
    for i in range(1, n_head):
        sums = sums + yrecv[i]
    mean = sums * (1.0 / full_width)
    inverse = lax.rsqrt(mean[:n_chunk] + EPSILON)
    slope = inverse * inverse * mean[n_chunk:]
    per_token = jnp.concatenate([inverse, slope], axis=0).T

    for j in range(n_chunk):
        inv_c = per_token[:, j : j + 1]
        slope_c = per_token[:, n_chunk + j : n_chunk + j + 1]
        for h in range(n_local):
            m = mixed[rows(j), cols(h)]
            gm_c = (inv_c * (g[rows(j), cols(h)].astype(F32) - m * slope_c)).astype(BF16)
            gm[rows(j), cols(h)] = gm_c
            o_v[rows(j), cols(h)] = (m * inv_c).astype(BF16)
            at = pl.ds(h * HEAD_DIM, HEAD_DIM)
            new = nn(qt[at, rows(j)], gm_c)
            gs_part[j, at, :] = new
            st[1, at, :] = new if j == 0 else st[1, at, :] + new
    core_copy(1, 0).start()
    out_o = pltpu.make_async_copy(o_v, o_hbm, out_sem.at[0])
    out_o.start()
    to_owners(1)

    @pl.loop(0, n_chunk)
    def _(j):
        for h in range(n_local):
            at = pl.ds(h * HEAD_DIM, HEAD_DIM)
            gm_c = gm[rows(j), cols(h)]
            before = (full[0, at, :] + cum[j, at, :]).astype(BF16)
            score = lower(nt(gm_c, v[rows(j), cols(h)]))
            gq_v[rows(j), cols(h)] = (nn(score, k[rows(j), cols(h)]) + nt(gm_c, before)).astype(BF16)

    from_owners(1)
    out_q = pltpu.make_async_copy(gq_v, gq_hbm, out_sem.at[1])
    out_q.start()

    for h in range(n_local):
        at = pl.ds(h * HEAD_DIM, HEAD_DIM)
        after = jnp.zeros((HEAD_DIM, HEAD_DIM), F32)
        for j in range(n_chunk - 1, -1, -1):
            new = gs_part[j, at, :]
            gs_part[j, at, :] = after
            after = after + new

    @pl.loop(0, n_chunk)
    def _(j):
        for h in range(n_local):
            at = pl.ds(h * HEAD_DIM, HEAD_DIM)
            gm_c, v_c, k_c = gm[rows(j), cols(h)], v[rows(j), cols(h)], k[rows(j), cols(h)]
            after = gs_part[j, at, :].astype(BF16)
            score = upper(nt(v_c, gm_c))
            gk_part[rows(j), cols(h)] = nn(score, q[rows(j), cols(h)]) + nt(v_c, after)
            gv_part[rows(j), cols(h)] = nn(score_t[j, h], gm_c) + nn(k_c, after)

    between_cores(1)
    core_copy(1, 1).wait_recv()
    fill_diag(1)
    for p in range(n_pair):
        for j in range(n_chunk):
            gk = gk_part[rows(j), pair_cols(p)] + nt(v[rows(j), pair_cols(p)], diag[1, p])
            gk_v[rows(j), pair_cols(p)] = gk.astype(BF16)
            gv = gv_part[rows(j), pair_cols(p)] + nn(k[rows(j), pair_cols(p)], diag[1, p])
            gv_v[rows(j), pair_cols(p)] = gv.astype(BF16)
    out_k = pltpu.make_async_copy(gk_v, gk_hbm, out_sem.at[2])
    out_v = pltpu.make_async_copy(gv_v, gv_hbm, out_sem.at[3])
    out_k.start()
    out_v.start()
    for copy in ycopies:
        copy.wait_send()
    for s in range(2):
        for stage in range(2):
            core_copy(s, stage).wait_send()
        wait_all(ps, s, b_send)
        wait_all(ds, s, d_send)
    for copy in (out_o, out_q, out_k, out_v):
        copy.wait()


def solution(mesh):
    chips_z = mesh.shape["seq"] // (2 * CHIPS_X)
    n_head = mesh.shape["head"]

    def shards(queries, keys, values, grad_out):
        tokens, width = queries.shape
        n_local = width // HEAD_DIM
        n_chunk = tokens // CHUNK
        n_chip = CHIPS_X * chips_z
        half = width // 2
        piece = half // n_chip
        wide = lambda dtype: pltpu.VMEM((tokens, width), dtype)
        scratch = [
            wide(BF16), wide(BF16), wide(BF16), wide(BF16),
            pltpu.VMEM((width, tokens), BF16),
            wide(F32),
            wide(BF16),
            pltpu.VMEM((n_chunk, n_local, CHUNK, CHUNK), BF16),
            wide(F32), wide(F32),
            wide(BF16), wide(BF16), wide(BF16), wide(BF16),
            pltpu.VMEM((n_chunk, width, HEAD_DIM), F32),
            pltpu.VMEM((n_chunk, width, HEAD_DIM), F32),
            pltpu.VMEM((2, width, HEAD_DIM), F32),
            pltpu.VMEM((2, half, HEAD_DIM), F32),
            pltpu.VMEM((2, n_chip, piece, HEAD_DIM), F32),
            pltpu.VMEM((2, n_chip, piece, HEAD_DIM), F32),
            pltpu.VMEM((2, n_chip, piece, HEAD_DIM), F32),
            pltpu.VMEM((2, n_chip, piece, HEAD_DIM), F32),
            pltpu.VMEM((2, half, HEAD_DIM), F32),
            pltpu.VMEM((2, width, HEAD_DIM), F32),
            pltpu.VMEM((2, n_local // 2, 2 * HEAD_DIM, 2 * HEAD_DIM), BF16),
            pltpu.VMEM((2 * n_chunk, CHUNK), F32),
            pltpu.VMEM((n_head, 2 * n_chunk, CHUNK), F32),
            pltpu.SemaphoreType.DMA((4,)),
            pltpu.SemaphoreType.DMA((4,)),
            pltpu.SemaphoreType.DMA((2, 2)),
            pltpu.SemaphoreType.DMA((2, 2)),
            pltpu.SemaphoreType.DMA((2,)),
            pltpu.SemaphoreType.DMA((2,)),
            pltpu.SemaphoreType.DMA((2,)),
            pltpu.SemaphoreType.DMA((2,)),
            pltpu.SemaphoreType.DMA((n_head - 1,)),
            pltpu.SemaphoreType.DMA,
        ]
        return pl.pallas_call(
            functools.partial(kernel, chips_z, n_head),
            out_shape=[jax.ShapeDtypeStruct((tokens, width), BF16)] * 4,
            in_specs=[pl.BlockSpec(memory_space=pl.ANY)] * 4,
            out_specs=[pl.BlockSpec(memory_space=pl.ANY)] * 4,
            scratch_shapes=scratch,
            compiler_params=pltpu.CompilerParams(
                collective_id=0, has_side_effects=True, vmem_limit_bytes=48 * 1024 * 1024
            ),
            cost_estimate=pl.CostEstimate(flops=4_000_000_000, bytes_accessed=8 << 20, transcendentals=4096),
        )(queries, keys, values, grad_out)

    spec = P("seq", "head")
    return jax.shard_map(
        shards, mesh=mesh, in_specs=(spec,) * 4, out_specs=(spec,) * 4, check_vma=False
    )
```

time: 404 us -> 54.1 us (0.13)
  waiting for transfers between devices: 176 us -> 0 us
  other arithmetic: 138 us -> 0 us
  Pallas kernels: 0 us -> 48.2 us
  matrix products: 35.3 us -> 0 us
  blocking collectives: 14.4 us -> 0 us
  between operations: 14.2 us -> 0.65 us
  local copies, waits for them, and re-layouts: 18.2 us -> 5.1 us
    all_gather x2 -> x0, waiting for transfers between devices: 176 us -> none  [entering(): everything = lax.all_gather(shard, axis)]
    select_n x128 -> x0, other arithmetic: 133 us -> none  [step(): return jnp.where(reached, new, before)]
    pallas_call x0 -> x1, Pallas kernels: none -> 48.2 us  [shards(): pl.pallas_call(functools.partial(kernel, chips_z, n_head), out_shape=[jax...]
    dot_general x12 -> x0, matrix products: 35.3 us -> none  [the longest x2 6.87 us: masked_scores(): jnp.einsum('thd,shd->hts', query_side, key_side, preferred_element_type=j...]
    psum x2 -> x0, blocking collectives: 14.4 us -> none  [the longest x1 8.42 us: shards(): squares = lax.psum(jnp.sum(mixed_rows * mixed_rows, axis=1), 'head')]
    unnamed x25 -> x6, local copies, waits for them, and re-layouts: 11.5 us -> 5.1 us
    reshape x3 -> x0, local copies, waits for them, and re-layouts: 5.81 us -> none  [the longest x1 2.4 us: shards(): key_rows = keys.reshape(shaped)]
  transfers between devices with their start and end apart: 2 -> 0, of which waited for: 2 -> 0; matrix products, arithmetic and copies ran while one was open for 6% -> 0% of each run, Pallas kernels for 0% -> 0%
where the time goes in v1:
time: 54.1 us; the launch traced here: 53.9 us
  Pallas kernels  48.2 us (89%)
  local copies, waits for them, and re-layouts  5.1 us (9%)
  between operations  0.65 us (1%)
    pallas_call x1, Pallas kernels, shards(): pl.pallas_call(functools.partial(kernel, chips_z, n_head), out_shape=[jax...  48.2 us
    unnamed x6, local copies, waits for them, and re-layouts  5.1 us

profile of v1, /device:TPU:1, one launch (start us, length us, event | category | flops | bytes accessed | tf_op | source)
XLA Modules:
  0.0 53.9 jit_solution(5167617644058182050)
XLA Ops:
  0.6 0.0 copy-start
  0.6 1.2 %copy-done = bf16[1024,512]{1,0:T(8,128)(2,1)S(1)} copy-done((bf16[1024,512]{1,0:T(8,128)(2,1)S(1)}, bf16[1024,512]{1,0:T(8,128)(2,1)}, u32[]{:S(2)}) %copy-start) | copy-done | bytes 1048600
  1.9 48.2 %shard_map.75 = (bf16[1024,512]{1,0:T(8,128)(2,1)S(1)}, bf16[1024,512]{1,0:T(8,128)(2,1)S(1)}, bf16[1024,512]{1,0:T(8,128)(2,1)S(1)}, bf16[1024,512]{1,0:T(8,128)(2,1)S(1)}) custom-call(bf16[1024,512]{1,0:T(8,128)(2,1)S(1)} %copy-done, bf16[1024,512]{1,0:T(8,128)(2,1)} %k_hbm.1, bf16[1024,512]{1,0:T(8,128)(2,1)} %v_hbm.1, bf16[1024,512]{1,0:T(8,128)(2,1)} %g_hbm.1), custom_call_target="tpu_custom_call" | custom-call | flops 4000000000 | bytes 8388608 | tf_op jit(solution)/shard_map/pallas_call | solution.py:349
  50.0 1.0 %copy.12 = bf16[1024,512]{1,0:T(8,128)(2,1)} copy(bf16[1024,512]{1,0:T(8,128)(2,1)S(1)} %get-tuple-element.8) | data formatting | bytes 2097152
  51.0 1.0 %copy.13 = bf16[1024,512]{1,0:T(8,128)(2,1)} copy(bf16[1024,512]{1,0:T(8,128)(2,1)S(1)} %get-tuple-element.9) | data formatting | bytes 2097152
  52.0 1.0 %copy.14 = bf16[1024,512]{1,0:T(8,128)(2,1)} copy(bf16[1024,512]{1,0:T(8,128)(2,1)S(1)} %get-tuple-element.10) | data formatting | bytes 2097152
  53.0 1.0 %copy.15 = bf16[1024,512]{1,0:T(8,128)(2,1)} copy(bf16[1024,512]{1,0:T(8,128)(2,1)S(1)} %get-tuple-element.11) | data formatting | bytes 2097152
Async XLA Ops:
  0.6 1.2 %copy-start = (bf16[1024,512]{1,0:T(8,128)(2,1)S(1)}, bf16[1024,512]{1,0:T(8,128)(2,1)}, u32[]{:S(2)}) copy-start(bf16[1024,512]{1,0:T(8,128)(2,1)} %q_hbm.1) | copy-start | bytes 3145732
